TPU v7x, 256 devices: a whole 4x4x8 slice. The times are simulated.
256 devices in a mesh: section: 4 (over x_lo, core), expert: 16 (over z, x_hi), tensor: 4 (over y).
Axes of the slice: x: 4 (x_hi: 2, x_lo: 2; x = x_hi * 2 + x_lo), y: 4, z: 8, core: 2. Of those that a mesh axis runs over, the one named last changes fastest.
Arguments:
- tokens: bfloat16 [4, 2048, 4096], P('section', 'expert', 'tensor'), may hold values from -6 to 6
- expert_ids: int32 [4, 2048, 8], P('section', 'expert'), may hold values from 0 to 15, all different within a row; in each aligned block of 128 rows (0 to 127, 128 to 255, ..., all dimensions but the last counted through in order) at most 72 rows name the same one
- gate_values: float32 [4, 2048, 8], P('section', 'expert'), may hold values from 0.05 to 0.5
- w_gate: bfloat16 [4, 16, 4096, 1536], P('section', 'expert', None, 'tensor'), may hold values from -0.09375 to 0.09375
- w_up: bfloat16 [4, 16, 4096, 1536], P('section', 'expert', None, 'tensor'), may hold values from -0.09375 to 0.09375
- w_down: bfloat16 [4, 16, 1536, 4096], P('section', 'expert', 'tensor'), may hold values from -0.15625 to 0.15625
Outputs:
- next_input: bfloat16 [4, 2048, 4096], P('section', 'expert', 'tensor')
Inputs may be any that keep to these rules, and one draw needn't show every extreme that they name: `expert_ids`: each row names 8 different experts. Among the rows of one index of the expert axis in one section, no expert is named more than 72 times, a bound that some block reaches.
All inputs are finite; a program needn't handle non-finite values.
Results may differ from a plain program's by a relative error of at most 0.0049.
Values may be sent and summed in bfloat16 or wider, within the bound.
A program may use at most 128 MiB of HBM per device.

v0:
```python
import jax
import jax.numpy as jnp
from jax import lax
from jax.sharding import PartitionSpec as P


def passed_along(x, axis, by):
    count = lax.axis_size(axis)
    return lax.ppermute(x, axis, [(i, (i + by) % count) for i in range(count)])


def on_device(tokens, expert_ids, gate_values, w_gate, w_up, w_down):
    own_part = tokens[0]
    pair_experts = expert_ids[0].reshape(-1)
    pair_gates = gate_values[0].reshape(-1)
    tok_rows, routed_per = (expert_ids.shape[1], expert_ids.shape[2])
    experts_here = w_gate.shape[1]
    peer_count = lax.axis_size("expert")
    total_experts = peer_count * experts_here
    capacity = min(tok_rows, tok_rows * routed_per * 9 // (8 * total_experts))
    onehot = (pair_experts[:, None] == jnp.arange(total_experts, dtype=jnp.int32)[None, :]).astype(
        jnp.int32
    )
    slot_index = jnp.sum((jnp.cumsum(onehot, axis=0) - 1) * onehot, axis=1)
    pair_token = jnp.arange(pair_experts.shape[0], dtype=jnp.int32) // routed_per
    whole_rows = lax.all_gather(own_part, "tensor", axis=1, tiled=True)
    row_width = whole_rows.shape[1]
    buffer = jnp.zeros((total_experts, capacity, row_width), jnp.bfloat16)
    buffer = buffer.at[pair_experts, slot_index].set(whole_rows[pair_token])
    arrived = lax.all_to_all(
        buffer.reshape(peer_count, experts_here, capacity, row_width),
        "expert",
        split_axis=0,
        concat_axis=0,
        tiled=True,
    )
    gate_act = jnp.einsum("sepd,edf->sepf", arrived, w_gate[0], preferred_element_type=jnp.float32)
    up_act = jnp.einsum("sepd,edf->sepf", arrived, w_up[0], preferred_element_type=jnp.float32)
    hidden = (jax.nn.silu(gate_act) * up_act).astype(jnp.bfloat16)
    partial_value = jnp.einsum(
        "sepf,efd->sepd", hidden, w_down[0], preferred_element_type=jnp.float32
    )
    shares = lax.psum_scatter(partial_value, "tensor", scatter_dimension=3, tiled=True)
    returned = lax.all_to_all(shares, "expert", split_axis=0, concat_axis=0, tiled=True)
    row_width = returned.shape[3]
    picked = returned.reshape(total_experts, capacity, row_width)[pair_experts, slot_index]
    combined = jnp.sum(
        (picked * pair_gates[:, None]).reshape(tok_rows, routed_per, row_width), axis=1
    )
    passed = passed_along(combined.astype(jnp.bfloat16)[None], "section", 1)
    return passed


def solution(mesh):
    in_specs = (
        P("section", "expert", "tensor"),
        P("section", "expert", None),
        P("section", "expert", None),
        P("section", "expert", None, "tensor"),
        P("section", "expert", None, "tensor"),
        P("section", "expert", "tensor", None),
    )
    out_specs = P("section", "expert", "tensor")
    return jax.shard_map(
        on_device, mesh=mesh, in_specs=in_specs, out_specs=out_specs, check_vma=False
    )
```

profile of v0, /device:TPU:1, one launch (start us, length us, event | category | flops | bytes accessed | tf_op | source)
XLA Modules:
  0.0 629.8 jit_solution(4022675972069388664)
XLA Ops:
  6.5 0.0 copy-start
  6.5 0.0 all-gather.3.cloned.1.call-start
  6.5 0.7 all-gather.3.cloned.1.call-update
  7.3 0.0 reduce-scatter.2.cloned.1.call-start
  7.3 1.0 copy.16
  8.3 0.1 eq.29
  8.4 0.1 eq.25
  8.5 0.1 reshape_squeeze.3
  8.6 4.5 reduce-window.6
  13.1 0.1 slice.12
  13.2 0.1 copy.19
  13.3 0.1 copy.20
  13.4 0.1 add_add_fusion
  13.6 0.7 multiply_reduce_fusion
  14.3 0.8 and_reduce_fusion
  15.1 23.6 %all-gather.3.cloned.1.call-done = bf16[1,128,4096]{2,1,0:T(8,128)(2,1)} async-done(((bf16[1,128,1024]{2,1,0:T(8,128)(2,1)}), bf16[1,128,4096]{2,1,0:T(8,128)(2,1)}) %all-gather.3.cloned.1.call-update) | async-done | bytes 1048592 | tf_op jit(solution)/shard_map/all_gather | solution.py:26
  38.6 16.4 %gather_fusion = bf16[1024,4096]{1,0:T(8,128)(2,1)} fusion(bf16[128,4096]{1,0:T(8,128)(2,1)} %bitcast.95, s32[1024]{0:T(1024)S(1)} %broadcast_clamp_fusion), kind=kCustom, calls=%fused_computation | custom fusion | bytes 16781312 | tf_op jit(solution)/shard_map/gather | solution.py:29
  55.1 18.2 %scatter_custom_fusion = bf16[1152,4096]{1,0:T(8,128)(2,1)} fusion(s32[1024]{0:T(1024)S(1)} %broadcast_select_fusion, bf16[1024,4096]{1,0:T(8,128)(2,1)} %gather_fusion, bf16[]{:T(256)} %constant.28.clone.1), kind=kCustom, calls=%fused_computation.8 | custom fusion | bytes 9437696
  73.3 0.0 copy-start.2
  73.3 217.0 %all_to_all.10 = bf16[16,1,72,4096]{3,2,1,0:T(8,128)(2,1)S(1)} all-to-all(bf16[16,1,72,4096]{3,2,1,0:T(8,128)(2,1)} %bitcast.97), channel_id=1, replica_groups=mesh['section'=4,'expert'=16,'tensor'=4] {'expert'}, dimensions={0} | all-to-all | bytes 18874368 | tf_op jit(solution)/shard_map/all_to_all | solution.py:30
  290.3 0.0 copy-done.2
  290.3 0.0 copy-start.3
  290.3 5.1 fusion.2
  295.4 0.0 copy-done.3
  295.4 5.2 fusion.18
  300.6 0.0 copy-done
  300.6 9.0 %convolution_bitcast_fusion = f32[16,1,72,4096]{3,2,0,1:T(8,128)} fusion(bf16[16,72,384]{2,1,0:T(8,128)(2,1)S(1)} %fusion.18, bf16[1,1,384,4096]{3,2,1,0:T(8,128)(2,1)S(1)} %copy-done), kind=kOutput, calls=%fused_computation.7 | convolution fusion | flops 3623878656 | bytes 22904832 | tf_op jit(solution)/shard_map/sepf,efd->sepd/dot_general | solution.py:40
  309.6 0.0 reduce-scatter.2.cloned.1.call-update
  309.6 164.1 %reduce-scatter.2.cloned.1.call-done = f32[16,1,72,1024]{3,2,0,1:T(8,128)} async-done(((f32[16,1,72,4096]{3,2,0,1:T(8,128)}), f32[16,1,72,1024]{3,2,0,1:T(8,128)}) %reduce-scatter.2.cloned.1.call-update) | async-done | bytes 4718608 | tf_op jit(solution)/shard_map/reduce_scatter | solution.py:43
  473.7 0.0 copy-start.1
  473.7 9.4 %all-to-all-start.1 = ((f32[16,1,72,1024]{3,2,1,0:T(8,128)}), f32[16,1,72,1024]{3,2,1,0:T(8,128)}, u32[]{:S(2)}, u32[]{:S(2)}) async-start(f32[16,1,72,1024]{3,2,1,0:T(8,128)} %bitcast.98), calls=%async_computation.2 | async-start | bytes 9437184 | tf_op jit(solution)/shard_map/all_to_all | solution.py:44
  483.2 0.0 copy-done.1
  483.2 0.1 copy.22
  483.3 110.0 %all-to-all-done.1 = f32[16,1,72,1024]{3,2,1,0:T(8,128)} async-done(((f32[16,1,72,1024]{3,2,1,0:T(8,128)}), f32[16,1,72,1024]{3,2,1,0:T(8,128)}, u32[]{:S(2)}, u32[]{:S(2)}) %all-to-all-start.1) | async-done | bytes 4718624 | tf_op jit(solution)/shard_map/all_to_all | solution.py:44
  593.3 20.5 %gather_fusion.1 = f32[1024,1024]{1,0:T(8,128)} fusion(f32[16,72,1024]{2,1,0:T(8,128)} %bitcast.26, s32[1024]{0:T(1024)S(1)} %bitcast.96), kind=kCustom, calls=%fused_computation.1 | custom fusion | bytes 8396800 | tf_op jit(solution)/shard_map/gather | solution.py:46
  613.8 3.5 fusion.6
  617.3 1.7 collective-permute-start
  619.0 3.3 collective-permute-done
  622.3 0.7 copy.26
  (8 shorter events, 0.1 us)
Async XLA Ops:
  6.5 294.1 %copy-start = (bf16[1,1,384,4096]{3,2,1,0:T(8,128)(2,1)S(1)}, bf16[1,1,384,4096]{3,2,1,0:T(8,128)(2,1)}, u32[]{:S(2)}) copy-start(bf16[1,1,384,4096]{3,2,1,0:T(8,128)(2,1)} %param.11) | copy-start | bytes 9437188
  6.5 32.1 %all-gather.3.cloned.1.call-start = ((), (), s32[]{:S(2)}) async-start(), calls=%async_computation.4 | async-start | bytes 1310720 | tf_op jit(solution)/shard_map/all_gather | solution.py:26
  7.3 466.5 %reduce-scatter.2.cloned.1.call-start = ((), (), s32[]{:S(2)}) async-start(), calls=%async_computation.3 | async-start | bytes 23592960 | tf_op jit(solution)/shard_map/reduce_scatter | solution.py:43
  73.3 217.0 %copy-start.2 = (bf16[1,1,4096,384]{3,2,1,0:T(8,128)(2,1)S(1)}, bf16[1,1,4096,384]{3,2,1,0:T(8,128)(2,1)}, u32[]{:S(2)}) copy-start(bf16[1,1,4096,384]{3,2,1,0:T(8,128)(2,1)} %param.9) | copy-start | bytes 9437188
  290.3 5.1 copy-start.3
  473.7 9.4 %copy-start.1 = (f32[1,128,8]{1,2,0:T(8,128)S(1)}, f32[1,128,8]{1,2,0:T(8,128)}, u32[]{:S(2)}) copy-start(f32[1,128,8]{1,2,0:T(8,128)} %param.8) | copy-start | bytes 12292
  473.7 119.6 %all-to-all-start.1 = ((f32[16,1,72,1024]{3,2,1,0:T(8,128)}), f32[16,1,72,1024]{3,2,1,0:T(8,128)}, u32[]{:S(2)}, u32[]{:S(2)}) async-start(f32[16,1,72,1024]{3,2,1,0:T(8,128)} %bitcast.98), calls=%async_computation.2 | async-start | bytes 9437184 | tf_op jit(solution)/shard_map/all_to_all | solution.py:44
  617.3 5.0 collective-permute-start
Sparse Core Ops, SparseCore 0:
  9.2 29.4 all-gather.2
  309.8 163.9 reduce-scatter.1
where the time goes:
time: 630 us
  waiting for transfers between devices  302 us (48%)
  blocking collectives  217 us (34%)
  local copies, waits for them, and re-layouts  57.5 us (9%)
  matrix products  19.3 us (3%)
  between operations  13.5 us (2%)
  starting transfers between devices  11.2 us (2%)
  other arithmetic  9.66 us (2%)
    all_to_all x1, blocking collectives, on_device(): lax.all_to_all(buffer.reshape(peer_count, experts_here, capacity, row_wid...  217 us
    reduce_scatter x1, waiting for transfers between devices, on_device(): lax.psum_scatter(partial_value, 'tensor', scatter_dimension=3, tiled=True)  164 us
    all_to_all x1, waiting for transfers between devices, on_device(): lax.all_to_all(shares, 'expert', split_axis=0, concat_axis=0, tiled=True)  110 us
    all_gather x1, waiting for transfers between devices, on_device(): whole_rows = lax.all_gather(own_part, 'tensor', axis=1, tiled=True)  23.6 us
    gather x1, local copies, waits for them, and re-layouts, on_device(): returned.reshape(total_experts, capacity, row_width)  20.5 us
    unnamed x11, local copies, waits for them, and re-layouts  19.9 us
    gather x1, local copies, waits for them, and re-layouts, on_device(): buffer = buffer.at[pair_experts, slot_index].set(whole_rows[pair_token])  16.4 us
  transfers between devices with their start and end apart: 4, of which 4 were waited for; matrix products, arithmetic and copies ran while one was open for 1% of the time, Pallas kernels for 0%

commit v1 on v0

v1 whole, which is shorter than its diff:
```python
import functools

import jax
import jax.numpy as jnp
from jax import lax
from jax.experimental import pallas as pl
from jax.experimental.pallas import tpu as pltpu
from jax.sharding import PartitionSpec as P

CAP = 72
PAD = 80
NAMES = 16
BF16 = jnp.bfloat16
F32 = jnp.float32


def iota(shape, dim):
    return lax.broadcasted_iota(jnp.int32, shape, dim)


def dot(a, b):
    return jnp.dot(a, b, preferred_element_type=F32)


def moe_kernel(
    nsec, nz, ny,
    tok_ref, ids_ref, gate_ref, wg_hbm, wu_hbm, wd_hbm, out_ref,
    wg, wu, wd, table, slot_t, tok2, xs, xg, slot_out, slot_in, xb, px, pr, x1, hidden,
    s1, r1, s2, r2, s3, r3, ret, back, mix, acc,
    w_sem, meta_send, meta_recv, tok_send, tok_recv, z_send, z_recv, slot_send, slot_recv,
    b1_send, b1_recv, b2_send, b2_recv, ring_send, ring_recv, tail_send, tail_recv, x_send, x_recv,
    g1_send, g1_recv, g2_send, g2_recv, r1_send, r1_recv, r2_send, r2_recv, r3_send, r3_recv,
    back_send, back_recv,
):
    sec, e, t = lax.axis_index("section"), lax.axis_index("expert"), lax.axis_index("tensor")
    z, xh = lax.div(e, 2), lax.rem(e, 2)
    rows, quarter = tok_ref.shape
    half = quarter // 2
    late = xg.shape[3]
    pair = 2 * CAP
    right, left, opposite = lax.rem(t + 1, ny), lax.rem(t + ny - 1, ny), lax.rem(t + 2, ny)
    after, before = lax.rem(sec + 1, nsec), lax.rem(sec + nsec - 1, nsec)

    def away(k):
        return lax.rem(lax.div(k + 1, 2) * (2 * lax.rem(k, 2) - 1) + nz, nz)

    def z_to(k):
        return lax.rem(z + away(k), nz)

    def z_from(k):
        return lax.rem(z - away(k) + nz, nz)

    loads = [
        pltpu.make_async_copy(wg_hbm, wg, w_sem.at[0]),
        pltpu.make_async_copy(wu_hbm, wu, w_sem.at[1]),
    ] + [
        pltpu.make_async_copy(wd_hbm.at[:, pl.ds(q * quarter, quarter)], wd.at[q], w_sem.at[2 + q])
        for q in range(ny)
    ]
    for load in loads:
        load.start()

    named = iota((NAMES, rows), 0)
    own = jnp.zeros((NAMES, rows), F32)
    for k in range(ids_ref.shape[0]):
        own = own + jnp.where(ids_ref[k : k + 1, :] == named, gate_ref[k : k + 1, :], 0.0)
    table[xh] = own

    barrier = pltpu.get_barrier_semaphore()

    def greet(device):
        pl.semaphore_signal(barrier, inc=1, device_id=device, device_id_type=pl.DeviceIdType.MESH)

    partner = (sec, z * 2 + 1 - xh, t)
    to_right, to_left = (sec, e, right), (sec, e, left)
    greet(to_right)
    greet(to_left)
    greet(partner)
    for k in range(1, nz):
        greet((sec, z_from(k) * 2 + xh, t))
    for other in range(2 * nz):
        greet((before, other, t))
    pl.semaphore_wait(barrier, (nz - 1) + 3 + 2 * nz)

    def push(src, dst, send, recv, device):
        return pltpu.make_async_remote_copy(
            src_ref=src, dst_ref=dst, send_sem=send, recv_sem=recv,
            device_id=device, device_id_type=pl.DeviceIdType.MESH,
        )

    def both_ways(a, b, send, recv, k):
        return (
            push(a[0], a[1], send.at[0, k], recv.at[0, k], to_right),
            push(b[0], b[1], send.at[1, k], recv.at[1, k], to_left),
        )

    def start(copies):
        for copy in copies:
            copy.start()

    def arrive(copies):
        for copy in copies:
            copy.wait_recv()

    def early_out():
        a = (tok_ref.at[:, pl.ds(late, quarter - late)], xb.at[0, t])
        return both_ways(a, a, b1_send, b1_recv, 0)

    def early_in():
        a, b = xb.at[0, left], xb.at[0, right]
        return both_ways((a, a), (b, b), b1_send, b1_recv, 0)

    def early_pass(from_left, from_right):
        a = xb.at[0, from_left, pl.ds(0, rows // 2)]
        b = xb.at[0, from_right, pl.ds(rows // 2, rows // 2)]
        return both_ways((a, a), (b, b), b2_send, b2_recv, 0)

    meta_x = push(table.at[xh], table.at[xh], meta_send.at[0], meta_recv.at[0], partner)
    meta_s = push(table.at[xh], table.at[2], meta_send.at[1], meta_recv.at[1], (after, e, t))
    late_part = tok_ref.at[:, pl.ds(0, late)]
    tok_x = push(late_part, tok2.at[xh], tok_send, tok_recv, partner)
    meta_x.start()
    tok_x.start()
    start(early_out())
    meta_s.start()
    tok2[xh] = tok_ref[:, :late]
    xb[0, t] = tok_ref[:, late:]

    earlier = (iota((rows, rows), 0) < iota((rows, rows), 1)).astype(BF16)

    def slots_by_expert(gates):
        names = (gates > 0).astype(F32)
        return jnp.where(names > 0, dot(names.astype(BF16), earlier), -1000.0)

    slot_t[xh] = slots_by_expert(own)
    push(table.at[1 - xh], table.at[1 - xh], meta_send.at[0], meta_recv.at[0], partner).wait_recv()
    slot_t[1 - xh] = slots_by_expert(table[1 - xh])
    arrive(early_in())
    start(early_pass(left, right))

    def to_z(k):
        return push(xs.at[k], xg.at[k, t], z_send.at[k], z_recv.at[k], (sec, z_to(k) * 2 + xh, t))

    def slots_to_z(k):
        return push(
            slot_out.at[k], slot_in.at[k], slot_send.at[k], slot_recv.at[k],
            (sec, z_to(k) * 2 + xh, t),
        )

    def picked(slots, shift, count):
        return (slots + shift == iota((count, rows), 0).astype(F32)).astype(BF16)

    def pick(k):
        expert = z_to(k) * 2 + xh
        chosen = [picked(slot_t[j, pl.ds(expert, 1), :], float(CAP * j), pair) for j in range(2)]
        return (dot(chosen[0], tok2[0]) + dot(chosen[1], tok2[1])).astype(BF16)

    def gather(k):
        a = xg.at[k, t]
        return both_ways((a, a), (a, a), g1_send, g1_recv, k)

    def gathered(k):
        a, b = xg.at[k, left], xg.at[k, right]
        return both_ways((a, a), (b, b), g1_send, g1_recv, k)

    def forward(k, from_left, from_right):
        a = xg.at[k, from_left, :, pl.ds(0, late // 2)]
        b = xg.at[k, from_right, :, pl.ds(late // 2, late // 2)]
        return both_ways((a, a), (b, b), g2_send, g2_recv, k)

    push(late_part, tok2.at[1 - xh], tok_send, tok_recv, partner).wait_recv()
    xg[0, t] = pick(0)
    start(gather(0))

    def ring_next(k):
        dz = 2 * lax.rem(k, 2) - 1
        device = (sec, lax.rem(z + dz + nz, nz) * 2 + xh, t)
        return push(xb.at[k], xb.at[k + 2], ring_send.at[k], ring_recv.at[k + 2], device)

    up_z, down_z = (sec, lax.rem(z + 1, nz) * 2 + xh, t), (sec, lax.rem(z + nz - 1, nz) * 2 + xh, t)

    def ring_first():
        return (
            push(xb.at[0], xb.at[1], ring_send.at[nz - 2], ring_recv.at[1], up_z),
            push(xb.at[0], xb.at[2], ring_send.at[nz - 1], ring_recv.at[2], down_z),
        )

    def ring_in(k):
        return push(xb.at[0], xb.at[k], ring_send.at[0], ring_recv.at[k], up_z)

    def ring_last(j):
        part = pl.ds(j * (ny // 2), ny // 2)
        return push(
            xb.at[nz - 3 + j, part], xb.at[nz - 1, part], tail_send.at[j], tail_recv.at[j],
            (up_z, down_z)[j],
        )

    def over_x(k):
        return push(px.at[k], pr.at[k], x_send.at[k], x_recv.at[k], partner)

    def pick_for_partner(k):
        chosen = picked(slot_in[k, pl.ds(1 - xh, 1), :], ((PAD - CAP) * xh).astype(F32), PAD)
        for q in range(ny):
            px[k, q] = dot(chosen, xb[k, q]).astype(BF16)
        over_x(k).start()

    slot_in[0, 0:1, :] = slot_t[xh, pl.ds(z * 2, 1), :]
    slot_in[0, 1:2, :] = slot_t[xh, pl.ds(z * 2 + 1, 1), :]
    arrive(early_pass(opposite, opposite))
    start(ring_first())

    def send_z(k, carry):
        xs[k] = pick(k)
        for j in range(2):
            slot_out[k, j : j + 1, :] = slot_t[xh, pl.ds(z_to(k) * 2 + j, 1), :]
        slots_to_z(k).start()
        to_z(k).start()
        return carry

    lax.fori_loop(1, nz, send_z, 0)
    pick_for_partner(0)

    push(table.at[2], table.at[2], meta_send.at[1], meta_recv.at[1], (after, e, t)).wait_recv()
    filler = jnp.zeros((128 - NAMES, rows), F32)
    gates = jnp.transpose(jnp.concatenate([table[2], filler], axis=0))
    slots = jnp.transpose(jnp.concatenate([slots_by_expert(table[2]), filler], axis=0))
    lanes = iota((rows, 128), 1)
    place = iota((rows, 2 * PAD), 1).astype(F32)

    def build_mix(k, carry):
        total = jnp.zeros((rows, 2 * PAD), F32)
        for j in range(2):
            here = lanes == z_to(k) * 2 + j
            gate = jnp.sum(jnp.where(here, gates, 0.0), axis=1, keepdims=True)
            slot = jnp.sum(jnp.where(here, slots, 0.0), axis=1, keepdims=True)
            at = slot + ((PAD - CAP) * xh).astype(F32) + float(PAD * j)
            total = total + jnp.where(place == at, gate, 0.0)
        high = total.astype(BF16)
        mix[k, 0] = high
        mix[k, 1] = (total - high.astype(F32)).astype(BF16)
        return carry

    lax.fori_loop(0, nz, build_mix, 0)
    acc[...] = jnp.zeros_like(acc)

    for load in loads:
        load.wait()

    def relay(k):
        return both_ways((s1.at[0, k], r1.at[0, k]), (s1.at[1, k], r1.at[1, k]), r1_send, r1_recv, k)

    def direct(k):
        return both_ways((s2.at[0, k], r2.at[0, k]), (s2.at[1, k], r2.at[1, k]), r2_send, r2_recv, k)

    def joined(k):
        return both_ways((s3.at[0, k], r3.at[0, k]), (s3.at[1, k], r3.at[1, k]), r3_send, r3_recv, k)

    def give_back(k):
        return tuple(
            push(
                ret.at[k, pl.ds((pair - PAD) * j, PAD)], back.at[k, pl.ds(PAD * xh, PAD)],
                back_send.at[j, k], back_recv.at[xh, k], (after, z_from(k) * 2 + j, t),
            )
            for j in range(2)
        )

    def given_back(k):
        return tuple(
            push(
                ret.at[k, pl.ds((pair - PAD) * j, PAD)], back.at[k, pl.ds(PAD * j, PAD)],
                back_send.at[j, k], back_recv.at[j, k], to_right,
            )
            for j in range(2)
        )

    def ring_stage(k):
        @pl.when(k < nz - 1)
        def _():
            ring_in(k).wait_recv()

        @pl.when(k < nz - 3)
        def _():
            ring_next(k).start()

        for j in range(2):
            @pl.when(k == nz - 3 + j)
            def _(j=j):
                ring_last(j).start()

        @pl.when(k == nz - 1)
        def _():
            ring_last(0).wait_recv()
            ring_last(1).wait_recv()

        slots_to_z(k).wait_recv()
        pick_for_partner(k)

    def gather_stage(k):
        push(xs.at[k], xg.at[k, t], z_send.at[k], z_recv.at[k], to_right).wait_recv()
        start(gather(k))

    def forward_stage(k):
        arrive(gathered(k))
        start(forward(k, left, right))

    def up_stage(k):
        arrive(forward(k, opposite, opposite))
        over_x(k).wait_recv()
        chosen = picked(slot_in[k, pl.ds(xh, 1), :], (CAP * xh).astype(F32), pair)
        theirs = pl.ds(pl.multiple_of((pair - PAD) * (1 - xh), 16), PAD)
        for q in range(ny):
            x1[q] = dot(chosen, xb[k, q]).astype(BF16)
            x1[q, theirs] = x1[q, theirs] + pr[k, q]
        gate_act = up_act = None
        for q in range(ny):
            for x, first, count in (
                (xg[k, q], q * quarter, late), (x1[q], q * quarter + late, quarter - late)
            ):
                g = dot(x, wg[first : first + count, :])
                u = dot(x, wu[first : first + count, :])
                gate_act = g if gate_act is None else gate_act + g
                up_act = u if up_act is None else up_act + u
        hidden[k] = (gate_act / (1.0 + jnp.exp(-gate_act)) * up_act).astype(BF16)
        part = dot(hidden[k], wd[opposite]).astype(BF16)
        s1[0, k] = part[:, :half]
        s1[1, k] = part[:, half:]
        start(relay(k))
        s2[0, k] = dot(hidden[k], wd[right, :, half:]).astype(BF16)
        s2[1, k] = dot(hidden[k], wd[left, :, :half]).astype(BF16)
        start(direct(k))

    def down_stage(k):
        arrive(relay(k))
        h = hidden[k]
        s3[0, k] = (dot(h, wd[right, :, :half]) + r1[0, k].astype(F32)).astype(BF16)
        s3[1, k] = (dot(h, wd[left, :, half:]) + r1[1, k].astype(F32)).astype(BF16)
        start(joined(k))

    def sum_stage(k):
        arrive(direct(k))
        arrive(joined(k))
        part = dot(hidden[k], wd[t])
        ret[k, :, :half] = (part[:, :half] + r3[0, k].astype(F32) + r2[1, k].astype(F32)).astype(BF16)
        ret[k, :, half:] = (part[:, half:] + r2[0, k].astype(F32) + r3[1, k].astype(F32)).astype(BF16)
        start(give_back(k))

    def mix_stage(k):
        arrive(given_back(k))
        y = back[k]
        acc[...] += dot(mix[k, 0], y) + dot(mix[k, 1], y)

    stages = (
        (-2, gather_stage, 1),
        (-2, ring_stage, 1),
        (-1, forward_stage, 0),
        (0, up_stage, 0),
        (1, down_stage, 0),
        (2, sum_stage, 0),
        (4, mix_stage, 0),
    )

    def step(i, carry):
        for lag, stage, first in stages:
            k = i - lag

            @pl.when((k >= first) & (k < nz))
            def _(stage=stage, k=k):
                stage(k)

        return carry

    lax.fori_loop(-1, nz + 4, step, 0)
    out_ref[...] = acc[...].astype(out_ref.dtype)

    def leave(copies):
        for copy in copies:
            copy.wait_send()

    leave((meta_x, meta_s, tok_x))
    leave(early_out())
    leave(early_pass(left, right))
    leave(ring_first())
    leave((ring_last(0), ring_last(1)))

    def drain(k, carry):
        @pl.when(k > 0)
        def _():
            leave((to_z(k), slots_to_z(k)))

        @pl.when((k > 0) & (k < nz - 3))
        def _():
            ring_next(k).wait_send()

        for copies in (
            gather(k), forward(k, left, right), relay(k), direct(k), joined(k), give_back(k),
        ):
            leave(copies)
        over_x(k).wait_send()
        return carry

    lax.fori_loop(0, nz, drain, 0)


def on_device(nsec, nz, ny, tokens, expert_ids, gate_values, w_gate, w_up, w_down):
    rows, quarter = tokens.shape[1:]
    width, units = w_gate.shape[2:]
    pair, half = 2 * CAP, quarter // 2
    late = 3 * quarter // 4
    early = quarter - late
    dma = pltpu.SemaphoreType.DMA
    vmem = lambda *shape, dtype=BF16: pltpu.VMEM(shape, dtype)
    sides = lambda n: [dma((2, n)), dma((2, n))]
    each = lambda n: [dma((n,)), dma((n,))]
    combined = pl.pallas_call(
        functools.partial(moe_kernel, nsec, nz, ny),
        out_shape=jax.ShapeDtypeStruct((rows, quarter), BF16),
        in_specs=[pl.BlockSpec(memory_space=pltpu.VMEM)] * 3 + [pl.BlockSpec(memory_space=pl.ANY)] * 3,
        out_specs=pl.BlockSpec(memory_space=pltpu.VMEM),
        scratch_shapes=[
            vmem(width, units), vmem(width, units), vmem(ny, units, quarter),
            vmem(3, NAMES, rows, dtype=F32),
            vmem(2, NAMES, rows, dtype=F32),
            vmem(2, rows, late),
            vmem(nz, pair, late),
            vmem(nz, ny, pair, late),
            vmem(nz, 8, rows, dtype=F32), vmem(nz, 8, rows, dtype=F32),
            vmem(nz, ny, rows, early),
            vmem(nz, ny, PAD, early), vmem(nz, ny, PAD, early),
            vmem(ny, pair, early),
            vmem(nz, pair, units),
            vmem(2, nz, pair, half), vmem(2, nz, pair, half),
            vmem(2, nz, pair, half), vmem(2, nz, pair, half),
            vmem(2, nz, pair, half), vmem(2, nz, pair, half),
            vmem(nz, pair, quarter),
            vmem(nz, 2 * PAD, quarter),
            vmem(nz, 2, rows, 2 * PAD),
            vmem(rows, quarter, dtype=F32),
            dma((2 + ny,)), *each(2), dma, dma, *each(nz), *each(nz),
            *sides(1), *sides(1), *each(nz), *each(2), *each(nz),
            *sides(nz), *sides(nz), *sides(nz), *sides(nz), *sides(nz),
            *sides(nz),
        ],
        compiler_params=pltpu.CompilerParams(
            collective_id=0, has_side_effects=True, vmem_limit_bytes=60 * 1024 * 1024
        ),
        cost_estimate=pl.CostEstimate(
            flops=6 * nz * pair * width * units, bytes_accessed=6 * width * units, transcendentals=0
        ),
    )(tokens[0], expert_ids[0].T, gate_values[0].T, w_gate[0, 0], w_up[0, 0], w_down[0, 0])
    return combined[None]


def solution(mesh):
    nsec, nexp, ny = mesh.shape["section"], mesh.shape["expert"], mesh.shape["tensor"]
    in_specs = (
        P("section", "expert", "tensor"),
        P("section", "expert", None),
        P("section", "expert", None),
        P("section", "expert", None, "tensor"),
        P("section", "expert", None, "tensor"),
        P("section", "expert", "tensor", None),
    )
    return jax.shard_map(
        functools.partial(on_device, nsec, nexp // 2, ny),
        mesh=mesh, in_specs=in_specs, out_specs=P("section", "expert", "tensor"), check_vma=False,
    )
```

time: 630 us -> 217 us (0.34)
  waiting for transfers between devices: 302 us -> 0 us
  blocking collectives: 217 us -> 0 us
  Pallas kernels: 0 us -> 215 us
  local copies, waits for them, and re-layouts: 57.5 us -> 1.67 us
  matrix products: 19.3 us -> 0 us
  between operations: 13.5 us -> 0.01 us
  starting transfers between devices: 11.2 us -> 0 us
  other arithmetic: 9.66 us -> 0 us
    all_to_all x1 -> x0, blocking collectives: 217 us -> none  [on_device(): lax.all_to_all(buffer.reshape(peer_count, experts_here, capacity, row_wid...]
    pallas_call x0 -> x1, Pallas kernels: none -> 215 us  [on_device(): pl.pallas_call(functools.partial(moe_kernel, nsec, nz, ny), out_shape=jax...]
    reduce_scatter x1 -> x0, waiting for transfers between devices: 164 us -> none  [on_device(): lax.psum_scatter(partial_value, 'tensor', scatter_dimension=3, tiled=True)]
    all_to_all x1 -> x0, waiting for transfers between devices: 110 us -> none  [on_device(): lax.all_to_all(shares, 'expert', split_axis=0, concat_axis=0, tiled=True)]
    gather x2 -> x0, local copies, waits for them, and re-layouts: 36.9 us -> none  [the longest x1 20.5 us: on_device(): returned.reshape(total_experts, capacity, row_width)]
    all_gather x1 -> x0, waiting for transfers between devices: 23.6 us -> none  [on_device(): whole_rows = lax.all_gather(own_part, 'tensor', axis=1, tiled=True)]
    dot_general x3 -> x0, matrix products: 19.3 us -> none  [the longest x1 8.98 us: on_device(): jnp.einsum('sepf,efd->sepd', hidden, w_down[0], preferred_element_type=jn...]
    unnamed x11 -> x1, local copies, waits for them, and re-layouts: 19.9 us -> 1.67 us
  transfers between devices with their start and end apart: 4 -> 0, of which waited for: 4 -> 0; matrix products, arithmetic and copies ran while one was open for 1% -> 0% of each run, Pallas kernels for 0% -> 0%
where the time goes in v1:
time: 217 us
  Pallas kernels  215 us (99%)
    pallas_call x1, Pallas kernels, on_device(): pl.pallas_call(functools.partial(moe_kernel, nsec, nz, ny), out_shape=jax...  215 us

profile of v1, /device:TPU:1, one launch (start us, length us, event | category | flops | bytes accessed | tf_op | source)
XLA Modules:
  0.0 216.5 jit_solution(5917356311084454481)
XLA Ops:
  0.0 214.8 %shard_map.64 = bf16[128,1024]{1,0:T(8,128)(2,1)} custom-call(bf16[128,1024]{1,0:T(8,128)(2,1)} %bitcast.15, s32[8,128]{1,0:T(8,128)} %bitcast.16, f32[8,128]{1,0:T(8,128)} %bitcast.17, bf16[4096,384]{1,0:T(8,128)(2,1)} %bitcast.12, bf16[4096,384]{1,0:T(8,128)(2,1)} %bitcast.13, bf16[384,4096]{1,0:T(8,128)(2,1)} %bitcast.14), custom_call_target="tpu_custom_call" | custom-call | flops 10871635968 | bytes 9437184 | tf_op jit(solution)/shard_map/pallas_call | solution.py:414
  214.9 1.7 copy.8

commit v2 on v1

--- a/solution.py
+++ b/solution.py
@@ -20,6 +20,10 @@
 
 def dot(a, b):
     return jnp.dot(a, b, preferred_element_type=F32)
+
+
+def order_of(nz):
+    return {2: (0, 1), 4: (0, 1, 3, 2), 8: (0, 1, 3, 6, 7, 5, 4, 2)}[nz]
 
 
 def moe_kernel(
@@ -50,6 +54,12 @@
     def z_from(k):
         return lax.rem(z - away(k) + nz, nz)
 
+    order = order_of(nz)
+    packed = sum(k << (3 * p) for p, k in enumerate(order))
+
+    def chunk_at(p):
+        return lax.rem(lax.shift_right_logical(packed, 3 * p), 8)
+
     loads = [
         pltpu.make_async_copy(wg_hbm, wg, w_sem.at[0]),
         pltpu.make_async_copy(wu_hbm, wu, w_sem.at[1]),
@@ -209,42 +219,48 @@
     arrive(early_pass(opposite, opposite))
     start(ring_first())
 
-    def send_z(k, carry):
+    def send_stage(k):
         xs[k] = pick(k)
+        to_z(k).start()
+
+    def send_slots(k, carry):
         for j in range(2):
             slot_out[k, j : j + 1, :] = slot_t[xh, pl.ds(z_to(k) * 2 + j, 1), :]
         slots_to_z(k).start()
-        to_z(k).start()
         return carry
 
-    lax.fori_loop(1, nz, send_z, 0)
+    for p in (1, 2):
+        if p < nz:
+            send_stage(jnp.int32(order[p]))
+    lax.fori_loop(1, nz, send_slots, 0)
     pick_for_partner(0)
-
-    push(table.at[2], table.at[2], meta_send.at[1], meta_recv.at[1], (after, e, t)).wait_recv()
-    filler = jnp.zeros((128 - NAMES, rows), F32)
-    gates = jnp.transpose(jnp.concatenate([table[2], filler], axis=0))
-    slots = jnp.transpose(jnp.concatenate([slots_by_expert(table[2]), filler], axis=0))
-    lanes = iota((rows, 128), 1)
-    place = iota((rows, 2 * PAD), 1).astype(F32)
-
-    def build_mix(k, carry):
-        total = jnp.zeros((rows, 2 * PAD), F32)
-        for j in range(2):
-            here = lanes == z_to(k) * 2 + j
-            gate = jnp.sum(jnp.where(here, gates, 0.0), axis=1, keepdims=True)
-            slot = jnp.sum(jnp.where(here, slots, 0.0), axis=1, keepdims=True)
-            at = slot + ((PAD - CAP) * xh).astype(F32) + float(PAD * j)
-            total = total + jnp.where(place == at, gate, 0.0)
-        high = total.astype(BF16)
-        mix[k, 0] = high
-        mix[k, 1] = (total - high.astype(F32)).astype(BF16)
-        return carry
-
-    lax.fori_loop(0, nz, build_mix, 0)
-    acc[...] = jnp.zeros_like(acc)
 
     for load in loads:
         load.wait()
+
+    def build_all_mix():
+        push(table.at[2], table.at[2], meta_send.at[1], meta_recv.at[1], (after, e, t)).wait_recv()
+        filler = jnp.zeros((128 - NAMES, rows), F32)
+        gates = jnp.transpose(jnp.concatenate([table[2], filler], axis=0))
+        slots = jnp.transpose(jnp.concatenate([slots_by_expert(table[2]), filler], axis=0))
+        lanes = iota((rows, 128), 1)
+        place = iota((rows, 2 * PAD), 1).astype(F32)
+
+        def build_mix(k, carry):
+            total = jnp.zeros((rows, 2 * PAD), F32)
+            for j in range(2):
+                here = lanes == z_to(k) * 2 + j
+                gate = jnp.sum(jnp.where(here, gates, 0.0), axis=1, keepdims=True)
+                slot = jnp.sum(jnp.where(here, slots, 0.0), axis=1, keepdims=True)
+                at = slot + ((PAD - CAP) * xh).astype(F32) + float(PAD * j)
+                total = total + jnp.where(place == at, gate, 0.0)
+            high = total.astype(BF16)
+            mix[k, 0] = high
+            mix[k, 1] = (total - high.astype(F32)).astype(BF16)
+            return carry
+
+        lax.fori_loop(0, nz, build_mix, 0)
+        acc[...] = jnp.zeros_like(acc)
 
     def relay(k):
         return both_ways((s1.at[0, k], r1.at[0, k]), (s1.at[1, k], r1.at[1, k]), r1_send, r1_recv, k)
@@ -349,32 +365,59 @@
         y = back[k]
         acc[...] += dot(mix[k, 0], y) + dot(mix[k, 1], y)
 
-    stages = (
-        (-2, gather_stage, 1),
-        (-2, ring_stage, 1),
-        (-1, forward_stage, 0),
-        (0, up_stage, 0),
-        (1, down_stage, 0),
-        (2, sum_stage, 0),
-        (4, mix_stage, 0),
-    )
-
-    def step(i, carry):
-        for lag, stage, first in stages:
-            k = i - lag
-
-            @pl.when((k >= first) & (k < nz))
-            def _(stage=stage, k=k):
-                stage(k)
-
-        return carry
-
-    lax.fori_loop(-1, nz + 4, step, 0)
-    out_ref[...] = acc[...].astype(out_ref.dtype)
-
     def leave(copies):
         for copy in copies:
             copy.wait_send()
+
+    def drain_stage(k):
+        @pl.when(k > 0)
+        def _():
+            leave((to_z(k), slots_to_z(k)))
+
+        @pl.when((k > 0) & (k < nz - 3))
+        def _():
+            ring_next(k).wait_send()
+
+        for copies in (
+            gather(k), forward(k, left, right), relay(k), direct(k), joined(k), give_back(k),
+        ):
+            leave(copies)
+        over_x(k).wait_send()
+
+    def staged(i, lag, stage, first):
+        p = i - lag
+
+        @pl.when((p >= first) & (p < nz))
+        def _():
+            stage(chunk_at(p))
+
+    def step(i, carry):
+        staged(i, -2, gather_stage, 1)
+        staged(i, -1, forward_stage, 0)
+        staged(i, 0, up_stage, 0)
+        staged(i, 1, down_stage, 0)
+
+        @pl.when((i >= 0) & (i < nz // 2))
+        def _():
+            ring_stage(2 * i + 1)
+
+        @pl.when((i >= 0) & (i < nz // 2 - 1))
+        def _():
+            ring_stage(2 * i + 2)
+
+        staged(i, -4, send_stage, 3)
+
+        @pl.when(i == 0)
+        def _():
+            build_all_mix()
+
+        staged(i, 2, sum_stage, 0)
+        staged(i, 4, mix_stage, 0)
+        staged(i, 5, drain_stage, 0)
+        return carry
+
+    lax.fori_loop(-1, nz + 5, step, 0)
+    out_ref[...] = acc[...].astype(out_ref.dtype)
 
     leave((meta_x, meta_s, tok_x))
     leave(early_out())
@@ -382,30 +425,12 @@
     leave(ring_first())
     leave((ring_last(0), ring_last(1)))
 
-    def drain(k, carry):
-        @pl.when(k > 0)
-        def _():
-            leave((to_z(k), slots_to_z(k)))
-
-        @pl.when((k > 0) & (k < nz - 3))
-        def _():
-            ring_next(k).wait_send()
-
-        for copies in (
-            gather(k), forward(k, left, right), relay(k), direct(k), joined(k), give_back(k),
-        ):
-            leave(copies)
-        over_x(k).wait_send()
-        return carry
-
-    lax.fori_loop(0, nz, drain, 0)
-
 
 def on_device(nsec, nz, ny, tokens, expert_ids, gate_values, w_gate, w_up, w_down):
     rows, quarter = tokens.shape[1:]
     width, units = w_gate.shape[2:]
     pair, half = 2 * CAP, quarter // 2
-    late = 3 * quarter // 4
+    late = quarter // 4
     early = quarter - late
     dma = pltpu.SemaphoreType.DMA
     vmem = lambda *shape, dtype=BF16: pltpu.VMEM(shape, dtype)

time: 217 us -> 203 us (0.935); the launches traced: 217 us -> 199 us
  Pallas kernels: 215 us -> 197 us
    pallas_call x1, Pallas kernels: 215 us -> 197 us  [on_device(): pl.pallas_call(functools.partial(moe_kernel, nsec, nz, ny), out_shape=jax...]
where the time goes in v2:
time: 203 us; the launch traced here: 199 us
  Pallas kernels  197 us (97%)
    pallas_call x1, Pallas kernels, on_device(): pl.pallas_call(functools.partial(moe_kernel, nsec, nz, ny), out_shape=jax...  197 us

profile of v2, /device:TPU:1, one launch (start us, length us, event | category | flops | bytes accessed | tf_op | source)
XLA Modules:
  0.0 199.2 jit_solution(15243953361999090026)
XLA Ops:
  0.0 197.5 %shard_map.64 = bf16[128,1024]{1,0:T(8,128)(2,1)} custom-call(bf16[128,1024]{1,0:T(8,128)(2,1)} %bitcast.15, s32[8,128]{1,0:T(8,128)} %bitcast.16, f32[8,128]{1,0:T(8,128)} %bitcast.17, bf16[4096,384]{1,0:T(8,128)(2,1)} %bitcast.12, bf16[4096,384]{1,0:T(8,128)(2,1)} %bitcast.13, bf16[384,4096]{1,0:T(8,128)(2,1)} %bitcast.14), custom_call_target="tpu_custom_call" | custom-call | flops 10871635968 | bytes 9437184 | tf_op jit(solution)/shard_map/pallas_call | solution.py:439
  197.5 1.7 copy.8

commit v3 on v2

--- a/solution.py
+++ b/solution.py
@@ -23,7 +23,7 @@
 
 
 def order_of(nz):
-    return {2: (0, 1), 4: (0, 1, 3, 2), 8: (0, 1, 3, 6, 7, 5, 4, 2)}[nz]
+    return {2: (0, 1), 4: (0, 1, 3, 2), 8: (0, 1, 4, 5, 6, 3, 7, 2)}[nz]
 
 
 def moe_kernel(
@@ -216,12 +216,16 @@
 
     slot_in[0, 0:1, :] = slot_t[xh, pl.ds(z * 2, 1), :]
     slot_in[0, 1:2, :] = slot_t[xh, pl.ds(z * 2 + 1, 1), :]
-    arrive(early_pass(opposite, opposite))
-    start(ring_first())
-
     def send_stage(k):
         xs[k] = pick(k)
         to_z(k).start()
+
+    for p in (1, 2):
+        if p < nz:
+            send_stage(jnp.int32(order[p]))
+
+    arrive(early_pass(opposite, opposite))
+    start(ring_first())
 
     def send_slots(k, carry):
         for j in range(2):
@@ -229,9 +233,6 @@
         slots_to_z(k).start()
         return carry
 
-    for p in (1, 2):
-        if p < nz:
-            send_stage(jnp.int32(order[p]))
     lax.fori_loop(1, nz, send_slots, 0)
     pick_for_partner(0)
 
@@ -308,6 +309,7 @@
             ring_last(0).wait_recv()
             ring_last(1).wait_recv()
 
+    def partner_stage(k):
         slots_to_z(k).wait_recv()
         pick_for_partner(k)
 
@@ -392,22 +394,23 @@
             stage(chunk_at(p))
 
     def step(i, carry):
+        staged(i, -1, forward_stage, 0)
         staged(i, -2, gather_stage, 1)
-        staged(i, -1, forward_stage, 0)
         staged(i, 0, up_stage, 0)
         staged(i, 1, down_stage, 0)
 
-        @pl.when((i >= 0) & (i < nz // 2))
-        def _():
-            ring_stage(2 * i + 1)
-
-        @pl.when((i >= 0) & (i < nz // 2 - 1))
-        def _():
-            ring_stage(2 * i + 2)
-
+        @pl.when(i < nz // 2 - 1)
+        def _():
+            ring_stage(2 * i + 3)
+
+        @pl.when(i < nz // 2 - 2)
+        def _():
+            ring_stage(2 * i + 4)
+
+        staged(i, -2, partner_stage, 1)
         staged(i, -4, send_stage, 3)
 
-        @pl.when(i == 0)
+        @pl.when(i == 1)
         def _():
             build_all_mix()
 
@@ -430,7 +433,7 @@
     rows, quarter = tokens.shape[1:]
     width, units = w_gate.shape[2:]
     pair, half = 2 * CAP, quarter // 2
-    late = quarter // 4
+    late = quarter // 2
     early = quarter - late
     dma = pltpu.SemaphoreType.DMA
     vmem = lambda *shape, dtype=BF16: pltpu.VMEM(shape, dtype)

time: 203 us -> 173 us (0.85); the launches traced: 199 us -> 172 us
  Pallas kernels: 197 us -> 171 us
    pallas_call x1, Pallas kernels: 197 us -> 171 us  [on_device(): pl.pallas_call(functools.partial(moe_kernel, nsec, nz, ny), out_shape=jax...]
where the time goes in v3:
time: 173 us; the launch traced here: 172 us
  Pallas kernels  171 us (99%)
    pallas_call x1, Pallas kernels, on_device(): pl.pallas_call(functools.partial(moe_kernel, nsec, nz, ny), out_shape=jax...  171 us

profile of v3, /device:TPU:1, one launch (start us, length us, event | category | flops | bytes accessed | tf_op | source)
XLA Modules:
  0.0 172.4 jit_solution(5038553437315056191)
XLA Ops:
  0.0 170.7 %shard_map.64 = bf16[128,1024]{1,0:T(8,128)(2,1)} custom-call(bf16[128,1024]{1,0:T(8,128)(2,1)} %bitcast.15, s32[8,128]{1,0:T(8,128)} %bitcast.16, f32[8,128]{1,0:T(8,128)} %bitcast.17, bf16[4096,384]{1,0:T(8,128)(2,1)} %bitcast.12, bf16[4096,384]{1,0:T(8,128)(2,1)} %bitcast.13, bf16[384,4096]{1,0:T(8,128)(2,1)} %bitcast.14), custom_call_target="tpu_custom_call" | custom-call | flops 10871635968 | bytes 9437184 | tf_op jit(solution)/shard_map/pallas_call | solution.py:442
  170.7 1.7 copy.8

commit v4 on v3

--- a/solution.py
+++ b/solution.py
@@ -23,7 +23,7 @@
 
 
 def order_of(nz):
-    return {2: (0, 1), 4: (0, 1, 3, 2), 8: (0, 1, 4, 5, 6, 3, 7, 2)}[nz]
+    return {2: (0, 1), 4: (0, 1, 3, 2), 8: (0, 1, 4, 5, 6, 7, 3, 2)}[nz]
 
 
 def moe_kernel(
@@ -394,10 +394,11 @@
             stage(chunk_at(p))
 
     def step(i, carry):
+        staged(i, 2, sum_stage, 0)
+        staged(i, 1, down_stage, 0)
         staged(i, -1, forward_stage, 0)
+        staged(i, 0, up_stage, 0)
         staged(i, -2, gather_stage, 1)
-        staged(i, 0, up_stage, 0)
-        staged(i, 1, down_stage, 0)
 
         @pl.when(i < nz // 2 - 1)
         def _():
@@ -414,7 +415,6 @@
         def _():
             build_all_mix()
 
-        staged(i, 2, sum_stage, 0)
         staged(i, 4, mix_stage, 0)
         staged(i, 5, drain_stage, 0)
         return carry

time: 173 us -> 168 us (0.971)
  Pallas kernels: 171 us -> 166 us
    pallas_call x1, Pallas kernels: 171 us -> 166 us  [on_device(): pl.pallas_call(functools.partial(moe_kernel, nsec, nz, ny), out_shape=jax...]
where the time goes in v4:
time: 168 us
  Pallas kernels  166 us (99%)
    pallas_call x1, Pallas kernels, on_device(): pl.pallas_call(functools.partial(moe_kernel, nsec, nz, ny), out_shape=jax...  166 us

profile of v4, /device:TPU:1, one launch (start us, length us, event | category | flops | bytes accessed | tf_op | source)
XLA Modules:
  0.0 168.0 jit_solution(12034025275197870708)
XLA Ops:
  0.0 166.3 %shard_map.64 = bf16[128,1024]{1,0:T(8,128)(2,1)} custom-call(bf16[128,1024]{1,0:T(8,128)(2,1)} %bitcast.15, s32[8,128]{1,0:T(8,128)} %bitcast.16, f32[8,128]{1,0:T(8,128)} %bitcast.17, bf16[4096,384]{1,0:T(8,128)(2,1)} %bitcast.12, bf16[4096,384]{1,0:T(8,128)(2,1)} %bitcast.13, bf16[384,4096]{1,0:T(8,128)(2,1)} %bitcast.14), custom_call_target="tpu_custom_call" | custom-call | flops 10871635968 | bytes 9437184 | tf_op jit(solution)/shard_map/pallas_call | solution.py:442
  166.3 1.7 copy.8

commit v5 on v4

--- a/solution.py
+++ b/solution.py
@@ -174,8 +174,8 @@
         return both_ways((a, a), (b, b), g1_send, g1_recv, k)
 
     def forward(k, from_left, from_right):
-        a = xg.at[k, from_left, :, pl.ds(0, late // 2)]
-        b = xg.at[k, from_right, :, pl.ds(late // 2, late // 2)]
+        a = xg.at[k, from_left, pl.ds(0, PAD)]
+        b = xg.at[k, from_right, pl.ds(PAD, pair - PAD)]
         return both_ways((a, a), (b, b), g2_send, g2_recv, k)
 
     push(late_part, tok2.at[1 - xh], tok_send, tok_recv, partner).wait_recv()
@@ -398,17 +398,17 @@
         staged(i, 1, down_stage, 0)
         staged(i, -1, forward_stage, 0)
         staged(i, 0, up_stage, 0)
+
+        @pl.when((i >= 0) & (i < nz // 2))
+        def _():
+            ring_stage(2 * i + 1)
+
+        @pl.when((i >= 0) & (i < nz // 2 - 1))
+        def _():
+            ring_stage(2 * i + 2)
+
+        staged(i, -1, partner_stage, 1)
         staged(i, -2, gather_stage, 1)
-
-        @pl.when(i < nz // 2 - 1)
-        def _():
-            ring_stage(2 * i + 3)
-
-        @pl.when(i < nz // 2 - 2)
-        def _():
-            ring_stage(2 * i + 4)
-
-        staged(i, -2, partner_stage, 1)
         staged(i, -4, send_stage, 3)
 
         @pl.when(i == 1)
@@ -433,7 +433,7 @@
     rows, quarter = tokens.shape[1:]
     width, units = w_gate.shape[2:]
     pair, half = 2 * CAP, quarter // 2
-    late = quarter // 2
+    late = 5 * quarter // 8
     early = quarter - late
     dma = pltpu.SemaphoreType.DMA
     vmem = lambda *shape, dtype=BF16: pltpu.VMEM(shape, dtype)

time: 168 us -> 165 us (0.982)
  Pallas kernels: 166 us -> 162 us
    pallas_call x1, Pallas kernels: 166 us -> 162 us  [on_device(): pl.pallas_call(functools.partial(moe_kernel, nsec, nz, ny), out_shape=jax...]
where the time goes in v5:
time: 165 us; the launch traced here: 164 us
  Pallas kernels  162 us (98%)
  local copies, waits for them, and re-layouts  1.67 us (1%)
    pallas_call x1, Pallas kernels, on_device(): pl.pallas_call(functools.partial(moe_kernel, nsec, nz, ny), out_shape=jax...  162 us

profile of v5, /device:TPU:1, one launch (start us, length us, event | category | flops | bytes accessed | tf_op | source)
XLA Modules:
  0.0 163.8 jit_solution(5563346673380669400)
XLA Ops:
  0.0 162.1 %shard_map.64 = bf16[128,1024]{1,0:T(8,128)(2,1)} custom-call(bf16[128,1024]{1,0:T(8,128)(2,1)} %bitcast.15, s32[8,128]{1,0:T(8,128)} %bitcast.16, f32[8,128]{1,0:T(8,128)} %bitcast.17, bf16[4096,384]{1,0:T(8,128)(2,1)} %bitcast.12, bf16[4096,384]{1,0:T(8,128)(2,1)} %bitcast.13, bf16[384,4096]{1,0:T(8,128)(2,1)} %bitcast.14), custom_call_target="tpu_custom_call" | custom-call | flops 10871635968 | bytes 9437184 | tf_op jit(solution)/shard_map/pallas_call | solution.py:442
  162.1 1.7 %copy.8 = bf16[1,128,1024]{2,1,0:T(8,128)(2,1)} copy(bf16[1,128,1024]{2,1,0:T(8,128)(2,1)} %bitcast.11) | data formatting | bytes 524288

commit v6 on v4

--- a/solution.py
+++ b/solution.py
@@ -174,8 +174,8 @@
         return both_ways((a, a), (b, b), g1_send, g1_recv, k)
 
     def forward(k, from_left, from_right):
-        a = xg.at[k, from_left, :, pl.ds(0, late // 2)]
-        b = xg.at[k, from_right, :, pl.ds(late // 2, late // 2)]
+        a = xg.at[k, from_left, pl.ds(0, PAD)]
+        b = xg.at[k, from_right, pl.ds(PAD, pair - PAD)]
         return both_ways((a, a), (b, b), g2_send, g2_recv, k)
 
     push(late_part, tok2.at[1 - xh], tok_send, tok_recv, partner).wait_recv()
@@ -396,30 +396,29 @@
     def step(i, carry):
         staged(i, 2, sum_stage, 0)
         staged(i, 1, down_stage, 0)
+        staged(i, 0, up_stage, 0)
         staged(i, -1, forward_stage, 0)
-        staged(i, 0, up_stage, 0)
+        staged(i, -4, send_stage, 3)
+
+        @pl.when(i == 1)
+        def _():
+            build_all_mix()
+
+        @pl.when(i < nz // 2 - 1)
+        def _():
+            ring_stage(2 * i + 3)
+
+        @pl.when(i < nz // 2 - 2)
+        def _():
+            ring_stage(2 * i + 4)
+
+        staged(i, -2, partner_stage, 1)
         staged(i, -2, gather_stage, 1)
-
-        @pl.when(i < nz // 2 - 1)
-        def _():
-            ring_stage(2 * i + 3)
-
-        @pl.when(i < nz // 2 - 2)
-        def _():
-            ring_stage(2 * i + 4)
-
-        staged(i, -2, partner_stage, 1)
-        staged(i, -4, send_stage, 3)
-
-        @pl.when(i == 1)
-        def _():
-            build_all_mix()
-
-        staged(i, 4, mix_stage, 0)
-        staged(i, 5, drain_stage, 0)
+        staged(i, 6, mix_stage, 0)
+        staged(i, 6, drain_stage, 0)
         return carry
 
-    lax.fori_loop(-1, nz + 5, step, 0)
+    lax.fori_loop(-1, nz + 6, step, 0)
     out_ref[...] = acc[...].astype(out_ref.dtype)
 
     leave((meta_x, meta_s, tok_x))

time: 168 us -> 173 us (1.030)
  Pallas kernels: 166 us -> 172 us
    pallas_call x1, Pallas kernels: 166 us -> 172 us  [on_device(): pl.pallas_call(functools.partial(moe_kernel, nsec, nz, ny), out_shape=jax...]
where the time goes in v6:
time: 173 us
  Pallas kernels  172 us (99%)
    pallas_call x1, Pallas kernels, on_device(): pl.pallas_call(functools.partial(moe_kernel, nsec, nz, ny), out_shape=jax...  172 us

profile of v6, /device:TPU:1, one launch (start us, length us, event | category | flops | bytes accessed | tf_op | source)
XLA Modules:
  0.0 173.2 jit_solution(9183620594388673739)
XLA Ops:
  0.0 171.6 %shard_map.64 = bf16[128,1024]{1,0:T(8,128)(2,1)} custom-call(bf16[128,1024]{1,0:T(8,128)(2,1)} %bitcast.15, s32[8,128]{1,0:T(8,128)} %bitcast.16, f32[8,128]{1,0:T(8,128)} %bitcast.17, bf16[4096,384]{1,0:T(8,128)(2,1)} %bitcast.12, bf16[4096,384]{1,0:T(8,128)(2,1)} %bitcast.13, bf16[384,4096]{1,0:T(8,128)(2,1)} %bitcast.14), custom_call_target="tpu_custom_call" | custom-call | flops 10871635968 | bytes 9437184 | tf_op jit(solution)/shard_map/pallas_call | solution.py:441
  171.6 1.7 copy.8

commit v7 on v5

--- a/solution.py
+++ b/solution.py
@@ -29,7 +29,7 @@
 def moe_kernel(
     nsec, nz, ny,
     tok_ref, ids_ref, gate_ref, wg_hbm, wu_hbm, wd_hbm, out_ref,
-    wg, wu, wd, table, slot_t, tok2, xs, xg, slot_out, slot_in, xb, px, pr, x1, hidden,
+    wgu, wd, table, slot_t, tok2, xs, xg, slot_out, slot_in, xb, px, pr, hidden,
     s1, r1, s2, r2, s3, r3, ret, back, mix, acc,
     w_sem, meta_send, meta_recv, tok_send, tok_recv, z_send, z_recv, slot_send, slot_recv,
     b1_send, b1_recv, b2_send, b2_recv, ring_send, ring_recv, tail_send, tail_recv, x_send, x_recv,
@@ -39,8 +39,8 @@
     sec, e, t = lax.axis_index("section"), lax.axis_index("expert"), lax.axis_index("tensor")
     z, xh = lax.div(e, 2), lax.rem(e, 2)
     rows, quarter = tok_ref.shape
-    half = quarter // 2
-    late = xg.shape[3]
+    half, units = quarter // 2, hidden.shape[2]
+    late = xs.shape[2]
     pair = 2 * CAP
     right, left, opposite = lax.rem(t + 1, ny), lax.rem(t + ny - 1, ny), lax.rem(t + 2, ny)
     after, before = lax.rem(sec + 1, nsec), lax.rem(sec + nsec - 1, nsec)
@@ -61,8 +61,8 @@
         return lax.rem(lax.shift_right_logical(packed, 3 * p), 8)
 
     loads = [
-        pltpu.make_async_copy(wg_hbm, wg, w_sem.at[0]),
-        pltpu.make_async_copy(wu_hbm, wu, w_sem.at[1]),
+        pltpu.make_async_copy(wg_hbm, wgu.at[:, pl.ds(0, units)], w_sem.at[0]),
+        pltpu.make_async_copy(wu_hbm, wgu.at[:, pl.ds(units, units)], w_sem.at[1]),
     ] + [
         pltpu.make_async_copy(wd_hbm.at[:, pl.ds(q * quarter, quarter)], wd.at[q], w_sem.at[2 + q])
         for q in range(ny)
@@ -148,8 +148,11 @@
     arrive(early_in())
     start(early_pass(left, right))
 
+    def late_of(k, q):
+        return xg.at[k, q, :, pl.ds(0, late)]
+
     def to_z(k):
-        return push(xs.at[k], xg.at[k, t], z_send.at[k], z_recv.at[k], (sec, z_to(k) * 2 + xh, t))
+        return push(xs.at[k], late_of(k, t), z_send.at[k], z_recv.at[k], (sec, z_to(k) * 2 + xh, t))
 
     def slots_to_z(k):
         return push(
@@ -166,20 +169,20 @@
         return (dot(chosen[0], tok2[0]) + dot(chosen[1], tok2[1])).astype(BF16)
 
     def gather(k):
-        a = xg.at[k, t]
+        a = late_of(k, t)
         return both_ways((a, a), (a, a), g1_send, g1_recv, k)
 
     def gathered(k):
-        a, b = xg.at[k, left], xg.at[k, right]
+        a, b = late_of(k, left), late_of(k, right)
         return both_ways((a, a), (b, b), g1_send, g1_recv, k)
 
     def forward(k, from_left, from_right):
-        a = xg.at[k, from_left, pl.ds(0, PAD)]
-        b = xg.at[k, from_right, pl.ds(PAD, pair - PAD)]
+        a = xg.at[k, from_left, pl.ds(0, PAD), pl.ds(0, late)]
+        b = xg.at[k, from_right, pl.ds(PAD, pair - PAD), pl.ds(0, late)]
         return both_ways((a, a), (b, b), g2_send, g2_recv, k)
 
     push(late_part, tok2.at[1 - xh], tok_send, tok_recv, partner).wait_recv()
-    xg[0, t] = pick(0)
+    xg[0, t, :, :late] = pick(0)
     start(gather(0))
 
     def ring_next(k):
@@ -314,7 +317,7 @@
         pick_for_partner(k)
 
     def gather_stage(k):
-        push(xs.at[k], xg.at[k, t], z_send.at[k], z_recv.at[k], to_right).wait_recv()
+        push(xs.at[k], late_of(k, t), z_send.at[k], z_recv.at[k], to_right).wait_recv()
         start(gather(k))
 
     def forward_stage(k):
@@ -327,17 +330,12 @@
         chosen = picked(slot_in[k, pl.ds(xh, 1), :], (CAP * xh).astype(F32), pair)
         theirs = pl.ds(pl.multiple_of((pair - PAD) * (1 - xh), 16), PAD)
         for q in range(ny):
-            x1[q] = dot(chosen, xb[k, q]).astype(BF16)
-            x1[q, theirs] = x1[q, theirs] + pr[k, q]
-        gate_act = up_act = None
-        for q in range(ny):
-            for x, first, count in (
-                (xg[k, q], q * quarter, late), (x1[q], q * quarter + late, quarter - late)
-            ):
-                g = dot(x, wg[first : first + count, :])
-                u = dot(x, wu[first : first + count, :])
-                gate_act = g if gate_act is None else gate_act + g
-                up_act = u if up_act is None else up_act + u
+            xg[k, q, :, late:] = dot(chosen, xb[k, q]).astype(BF16)
+            xg[k, q, theirs, late:] = xg[k, q, theirs, late:] + pr[k, q]
+        acts = dot(xg[k, 0], wgu[:quarter, :])
+        for q in range(1, ny):
+            acts = acts + dot(xg[k, q], wgu[q * quarter : (q + 1) * quarter, :])
+        gate_act, up_act = acts[:, :units], acts[:, units:]
         hidden[k] = (gate_act / (1.0 + jnp.exp(-gate_act)) * up_act).astype(BF16)
         part = dot(hidden[k], wd[opposite]).astype(BF16)
         s1[0, k] = part[:, :half]
@@ -445,16 +443,15 @@
         in_specs=[pl.BlockSpec(memory_space=pltpu.VMEM)] * 3 + [pl.BlockSpec(memory_space=pl.ANY)] * 3,
         out_specs=pl.BlockSpec(memory_space=pltpu.VMEM),
         scratch_shapes=[
-            vmem(width, units), vmem(width, units), vmem(ny, units, quarter),
+            vmem(width, 2 * units), vmem(ny, units, quarter),
             vmem(3, NAMES, rows, dtype=F32),
             vmem(2, NAMES, rows, dtype=F32),
             vmem(2, rows, late),
             vmem(nz, pair, late),
-            vmem(nz, ny, pair, late),
+            vmem(nz, ny, pair, quarter),
             vmem(nz, 8, rows, dtype=F32), vmem(nz, 8, rows, dtype=F32),
             vmem(nz, ny, rows, early),
             vmem(nz, ny, PAD, early), vmem(nz, ny, PAD, early),
-            vmem(ny, pair, early),
             vmem(nz, pair, units),
             vmem(2, nz, pair, half), vmem(2, nz, pair, half),
             vmem(2, nz, pair, half), vmem(2, nz, pair, half),

time: 165 us -> 165 us (level)
  no operation moved by 1% of the time
where the time goes in v7:
time: 165 us; the launch traced here: 164 us
  Pallas kernels  162 us (98%)
  local copies, waits for them, and re-layouts  1.67 us (1%)
    pallas_call x1, Pallas kernels, on_device(): pl.pallas_call(functools.partial(moe_kernel, nsec, nz, ny), out_shape=jax...  162 us

profile of v7, /device:TPU:1, one launch (start us, length us, event | category | flops | bytes accessed | tf_op | source)
XLA Modules:
  0.0 163.7 jit_solution(3447375724014878038)
XLA Ops:
  0.0 162.0 %shard_map.64 = bf16[128,1024]{1,0:T(8,128)(2,1)} custom-call(bf16[128,1024]{1,0:T(8,128)(2,1)} %bitcast.15, s32[8,128]{1,0:T(8,128)} %bitcast.16, f32[8,128]{1,0:T(8,128)} %bitcast.17, bf16[4096,384]{1,0:T(8,128)(2,1)} %bitcast.12, bf16[4096,384]{1,0:T(8,128)(2,1)} %bitcast.13, bf16[384,4096]{1,0:T(8,128)(2,1)} %bitcast.14), custom_call_target="tpu_custom_call" | custom-call | flops 10871635968 | bytes 9437184 | tf_op jit(solution)/shard_map/pallas_call | solution.py:440
  162.0 1.7 %copy.8 = bf16[1,128,1024]{2,1,0:T(8,128)(2,1)} copy(bf16[1,128,1024]{2,1,0:T(8,128)(2,1)} %bitcast.11) | data formatting | bytes 524288

commit v8 on v7

--- a/solution.py
+++ b/solution.py
@@ -8,7 +8,8 @@
 from jax.sharding import PartitionSpec as P
 
 CAP = 72
-PAD = 80
+MAIN = 64
+TAIL = CAP - MAIN
 NAMES = 16
 BF16 = jnp.bfloat16
 F32 = jnp.float32
@@ -42,6 +43,7 @@
     half, units = quarter // 2, hidden.shape[2]
     late = xs.shape[2]
     pair = 2 * CAP
+    packed_rows = ny * MAIN
     right, left, opposite = lax.rem(t + 1, ny), lax.rem(t + ny - 1, ny), lax.rem(t + 2, ny)
     after, before = lax.rem(sec + 1, nsec), lax.rem(sec + nsec - 1, nsec)
 
@@ -177,8 +179,9 @@
         return both_ways((a, a), (b, b), g1_send, g1_recv, k)
 
     def forward(k, from_left, from_right):
-        a = xg.at[k, from_left, pl.ds(0, PAD), pl.ds(0, late)]
-        b = xg.at[k, from_right, pl.ds(PAD, pair - PAD), pl.ds(0, late)]
+        split = MAIN + 2 * TAIL
+        a = xg.at[k, from_left, pl.ds(0, split), pl.ds(0, late)]
+        b = xg.at[k, from_right, pl.ds(split, pair - split), pl.ds(0, late)]
         return both_ways((a, a), (b, b), g2_send, g2_recv, k)
 
     push(late_part, tok2.at[1 - xh], tok_send, tok_recv, partner).wait_recv()
@@ -212,9 +215,18 @@
         return push(px.at[k], pr.at[k], x_send.at[k], x_recv.at[k], partner)
 
     def pick_for_partner(k):
-        chosen = picked(slot_in[k, pl.ds(1 - xh, 1), :], ((PAD - CAP) * xh).astype(F32), PAD)
+        slots = slot_in[k, pl.ds(1 - xh, 1), :]
+        main = picked(slots, (-TAIL * xh).astype(F32), MAIN)
+        low = iota((2 * TAIL, rows), 0) < TAIL
+        tail = picked(slots, (-MAIN * (1 - xh)).astype(F32), 2 * TAIL)
+        tail_up = picked(slots, (TAIL - MAIN * (1 - xh)).astype(F32), 2 * TAIL)
+        tails = (jnp.where(low, tail, 0).astype(BF16), jnp.where(low, 0, tail_up).astype(BF16))
         for q in range(ny):
-            px[k, q] = dot(chosen, xb[k, q]).astype(BF16)
+            px[k, q * MAIN : (q + 1) * MAIN] = dot(main, xb[k, q]).astype(BF16)
+        for j in range(ny // 2):
+            both = dot(tails[0], xb[k, 2 * j]) + dot(tails[1], xb[k, 2 * j + 1])
+            first = packed_rows + j * 2 * TAIL
+            px[k, first : first + 2 * TAIL] = both.astype(BF16)
         over_x(k).start()
 
     slot_in[0, 0:1, :] = slot_t[xh, pl.ds(z * 2, 1), :]
@@ -248,19 +260,24 @@
         gates = jnp.transpose(jnp.concatenate([table[2], filler], axis=0))
         slots = jnp.transpose(jnp.concatenate([slots_by_expert(table[2]), filler], axis=0))
         lanes = iota((rows, 128), 1)
-        place = iota((rows, 2 * PAD), 1).astype(F32)
+        place = iota((rows, 2 * pair), 1).astype(F32)
 
         def build_mix(k, carry):
-            total = jnp.zeros((rows, 2 * PAD), F32)
+            total = [jnp.zeros((rows, 2 * pair), F32) for _ in range(2)]
             for j in range(2):
                 here = lanes == z_to(k) * 2 + j
                 gate = jnp.sum(jnp.where(here, gates, 0.0), axis=1, keepdims=True)
                 slot = jnp.sum(jnp.where(here, slots, 0.0), axis=1, keepdims=True)
-                at = slot + ((PAD - CAP) * xh).astype(F32) + float(PAD * j)
-                total = total + jnp.where(place == at, gate, 0.0)
-            high = total.astype(BF16)
-            mix[k, 0] = high
-            mix[k, 1] = (total - high.astype(F32)).astype(BF16)
+                main = slot - (TAIL * xh).astype(F32)
+                tail = slot - (MAIN * (1 - xh)).astype(F32)
+                in_main = (main >= 0) & (main < MAIN)
+                for side in range(2):
+                    at = jnp.where(in_main, main + MAIN * side, tail + (2 * MAIN + TAIL * side))
+                    total[side] = total[side] + jnp.where(place == at + pair * j, gate, 0.0)
+            for side in range(2):
+                high = total[side].astype(BF16)
+                mix[k, side, 0] = high
+                mix[k, side, 1] = (total[side] - high.astype(F32)).astype(BF16)
             return carry
 
         lax.fori_loop(0, nz, build_mix, 0)
@@ -278,7 +295,7 @@
     def give_back(k):
         return tuple(
             push(
-                ret.at[k, pl.ds((pair - PAD) * j, PAD)], back.at[k, pl.ds(PAD * xh, PAD)],
+                ret.at[k, j], back.at[k, pl.ds(pair * xh, pair)],
                 back_send.at[j, k], back_recv.at[xh, k], (after, z_from(k) * 2 + j, t),
             )
             for j in range(2)
@@ -287,7 +304,7 @@
     def given_back(k):
         return tuple(
             push(
-                ret.at[k, pl.ds((pair - PAD) * j, PAD)], back.at[k, pl.ds(PAD * j, PAD)],
+                ret.at[k, j], back.at[k, pl.ds(pair * j, pair)],
                 back_send.at[j, k], back_recv.at[j, k], to_right,
             )
             for j in range(2)
@@ -328,10 +345,17 @@
         arrive(forward(k, opposite, opposite))
         over_x(k).wait_recv()
         chosen = picked(slot_in[k, pl.ds(xh, 1), :], (CAP * xh).astype(F32), pair)
-        theirs = pl.ds(pl.multiple_of((pair - PAD) * (1 - xh), 16), PAD)
+        theirs = pl.ds(pl.multiple_of((MAIN + 2 * TAIL) * (1 - xh), 16), MAIN)
+        middle = slice(MAIN, MAIN + 2 * TAIL)
+        r, c = iota((2 * TAIL, 2 * TAIL), 0), iota((2 * TAIL, 2 * TAIL), 1)
+        mine = (r < TAIL) == (xh == 1)
         for q in range(ny):
             xg[k, q, :, late:] = dot(chosen, xb[k, q]).astype(BF16)
-            xg[k, q, theirs, late:] = xg[k, q, theirs, late:] + pr[k, q]
+            xg[k, q, theirs, late:] = pr[k, q * MAIN : (q + 1) * MAIN]
+            shift = (mine & (c == r + TAIL * (q % 2) - TAIL * (1 - xh))).astype(BF16)
+            first = packed_rows + (q // 2) * 2 * TAIL
+            moved = dot(shift, pr[k, first : first + 2 * TAIL]).astype(BF16)
+            xg[k, q, middle, late:] = xg[k, q, middle, late:] + moved
         acts = dot(xg[k, 0], wgu[:quarter, :])
         for q in range(1, ny):
             acts = acts + dot(xg[k, q], wgu[q * quarter : (q + 1) * quarter, :])
@@ -356,14 +380,21 @@
         arrive(direct(k))
         arrive(joined(k))
         part = dot(hidden[k], wd[t])
-        ret[k, :, :half] = (part[:, :half] + r3[0, k].astype(F32) + r2[1, k].astype(F32)).astype(BF16)
-        ret[k, :, half:] = (part[:, half:] + r2[0, k].astype(F32) + r3[1, k].astype(F32)).astype(BF16)
+        lo = part[:, :half] + r3[0, k].astype(F32) + r2[1, k].astype(F32)
+        hi = part[:, half:] + r2[0, k].astype(F32) + r3[1, k].astype(F32)
+        for j in range(2):
+            first, tail = (MAIN + 2 * TAIL) * j, MAIN + TAIL * j
+            ret[k, j, :MAIN] = lo[first : first + MAIN].astype(BF16)
+            ret[k, j, MAIN : 2 * MAIN] = hi[first : first + MAIN].astype(BF16)
+            tails = jnp.concatenate([lo[tail : tail + TAIL], hi[tail : tail + TAIL]], axis=0)
+            ret[k, j, 2 * MAIN :] = tails.astype(BF16)
         start(give_back(k))
 
     def mix_stage(k):
         arrive(given_back(k))
         y = back[k]
-        acc[...] += dot(mix[k, 0], y) + dot(mix[k, 1], y)
+        acc[:, :half] += dot(mix[k, 0, 0], y) + dot(mix[k, 0, 1], y)
+        acc[:, half:] += dot(mix[k, 1, 0], y) + dot(mix[k, 1, 1], y)
 
     def leave(copies):
         for copy in copies:
@@ -451,14 +482,14 @@
             vmem(nz, ny, pair, quarter),
             vmem(nz, 8, rows, dtype=F32), vmem(nz, 8, rows, dtype=F32),
             vmem(nz, ny, rows, early),
-            vmem(nz, ny, PAD, early), vmem(nz, ny, PAD, early),
+            vmem(nz, ny * CAP, early), vmem(nz, ny * CAP, early),
             vmem(nz, pair, units),
             vmem(2, nz, pair, half), vmem(2, nz, pair, half),
             vmem(2, nz, pair, half), vmem(2, nz, pair, half),
             vmem(2, nz, pair, half), vmem(2, nz, pair, half),
-            vmem(nz, pair, quarter),
-            vmem(nz, 2 * PAD, quarter),
-            vmem(nz, 2, rows, 2 * PAD),
+            vmem(nz, 2, pair, half),
+            vmem(nz, 2 * pair, half),
+            vmem(nz, 2, 2, rows, 2 * pair),
             vmem(rows, quarter, dtype=F32),
             dma((2 + ny,)), *each(2), dma, dma, *each(nz), *each(nz),
             *sides(1), *sides(1), *each(nz), *each(2), *each(nz),

time: 165 us -> 163 us (0.988)
  no operation moved by 1% of the time
where the time goes in v8:
time: 163 us
  Pallas kernels  162 us (99%)
  local copies, waits for them, and re-layouts  1.67 us (1%)
    pallas_call x1, Pallas kernels, on_device(): pl.pallas_call(functools.partial(moe_kernel, nsec, nz, ny), out_shape=jax...  162 us

profile of v8, /device:TPU:1, one launch (start us, length us, event | category | flops | bytes accessed | tf_op | source)
XLA Modules:
  0.0 163.2 jit_solution(7678179526606078926)
XLA Ops:
  0.0 161.5 %shard_map.64 = bf16[128,1024]{1,0:T(8,128)(2,1)} custom-call(bf16[128,1024]{1,0:T(8,128)(2,1)} %bitcast.15, s32[8,128]{1,0:T(8,128)} %bitcast.16, f32[8,128]{1,0:T(8,128)} %bitcast.17, bf16[4096,384]{1,0:T(8,128)(2,1)} %bitcast.12, bf16[4096,384]{1,0:T(8,128)(2,1)} %bitcast.13, bf16[384,4096]{1,0:T(8,128)(2,1)} %bitcast.14), custom_call_target="tpu_custom_call" | custom-call | flops 10871635968 | bytes 9437184 | tf_op jit(solution)/shard_map/pallas_call | solution.py:471
  161.5 1.7 %copy.8 = bf16[1,128,1024]{2,1,0:T(8,128)(2,1)} copy(bf16[1,128,1024]{2,1,0:T(8,128)(2,1)} %bitcast.11) | data formatting | bytes 524288

commit v9 on v8

--- a/solution.py
+++ b/solution.py
@@ -31,7 +31,7 @@
     nsec, nz, ny,
     tok_ref, ids_ref, gate_ref, wg_hbm, wu_hbm, wd_hbm, out_ref,
     wgu, wd, table, slot_t, tok2, xs, xg, slot_out, slot_in, xb, px, pr, hidden,
-    s1, r1, s2, r2, s3, r3, ret, back, mix, acc,
+    s1, r1, s2, r2, s3, r3, ret, back, turned, mix, acc,
     w_sem, meta_send, meta_recv, tok_send, tok_recv, z_send, z_recv, slot_send, slot_recv,
     b1_send, b1_recv, b2_send, b2_recv, ring_send, ring_recv, tail_send, tail_recv, x_send, x_recv,
     g1_send, g1_recv, g2_send, g2_recv, r1_send, r1_recv, r2_send, r2_recv, r3_send, r3_recv,
@@ -254,34 +254,31 @@
     for load in loads:
         load.wait()
 
-    def build_all_mix():
+    def turn_tables():
         push(table.at[2], table.at[2], meta_send.at[1], meta_recv.at[1], (after, e, t)).wait_recv()
         filler = jnp.zeros((128 - NAMES, rows), F32)
-        gates = jnp.transpose(jnp.concatenate([table[2], filler], axis=0))
-        slots = jnp.transpose(jnp.concatenate([slots_by_expert(table[2]), filler], axis=0))
+        turned[0] = jnp.transpose(jnp.concatenate([table[2], filler], axis=0))
+        turned[1] = jnp.transpose(jnp.concatenate([slots_by_expert(table[2]), filler], axis=0))
+        acc[...] = jnp.zeros_like(acc)
+
+    def weight_stage(k):
         lanes = iota((rows, 128), 1)
         place = iota((rows, 2 * pair), 1).astype(F32)
-
-        def build_mix(k, carry):
-            total = [jnp.zeros((rows, 2 * pair), F32) for _ in range(2)]
-            for j in range(2):
-                here = lanes == z_to(k) * 2 + j
-                gate = jnp.sum(jnp.where(here, gates, 0.0), axis=1, keepdims=True)
-                slot = jnp.sum(jnp.where(here, slots, 0.0), axis=1, keepdims=True)
-                main = slot - (TAIL * xh).astype(F32)
-                tail = slot - (MAIN * (1 - xh)).astype(F32)
-                in_main = (main >= 0) & (main < MAIN)
-                for side in range(2):
-                    at = jnp.where(in_main, main + MAIN * side, tail + (2 * MAIN + TAIL * side))
-                    total[side] = total[side] + jnp.where(place == at + pair * j, gate, 0.0)
+        total = [jnp.zeros((rows, 2 * pair), F32) for _ in range(2)]
+        for j in range(2):
+            here = lanes == z_to(k) * 2 + j
+            gate = jnp.sum(jnp.where(here, turned[0], 0.0), axis=1, keepdims=True)
+            slot = jnp.sum(jnp.where(here, turned[1], 0.0), axis=1, keepdims=True)
+            main = slot - (TAIL * xh).astype(F32)
+            tail = slot - (MAIN * (1 - xh)).astype(F32)
+            in_main = (main >= 0) & (main < MAIN)
             for side in range(2):
-                high = total[side].astype(BF16)
-                mix[k, side, 0] = high
-                mix[k, side, 1] = (total[side] - high.astype(F32)).astype(BF16)
-            return carry
-
-        lax.fori_loop(0, nz, build_mix, 0)
-        acc[...] = jnp.zeros_like(acc)
+                at = jnp.where(in_main, main + MAIN * side, tail + (2 * MAIN + TAIL * side))
+                total[side] = total[side] + jnp.where(place == at + pair * j, gate, 0.0)
+        for side in range(2):
+            high = total[side].astype(BF16)
+            mix[k, side, 0] = high
+            mix[k, side, 1] = (total[side] - high.astype(F32)).astype(BF16)
 
     def relay(k):
         return both_ways((s1.at[0, k], r1.at[0, k]), (s1.at[1, k], r1.at[1, k]), r1_send, r1_recv, k)
@@ -426,24 +423,25 @@
         staged(i, 2, sum_stage, 0)
         staged(i, 1, down_stage, 0)
         staged(i, -1, forward_stage, 0)
+
+        def ring_and_partner():
+            @pl.when(i < nz // 2)
+            def _():
+                ring_stage(2 * i + 1)
+
+            @pl.when(i < nz // 2 - 1)
+            def _():
+                ring_stage(2 * i + 2)
+
+            staged(i, -1, partner_stage, 1)
+
+        pl.when(i > 0)(ring_and_partner)
         staged(i, 0, up_stage, 0)
-
-        @pl.when((i >= 0) & (i < nz // 2))
-        def _():
-            ring_stage(2 * i + 1)
-
-        @pl.when((i >= 0) & (i < nz // 2 - 1))
-        def _():
-            ring_stage(2 * i + 2)
-
-        staged(i, -1, partner_stage, 1)
+        pl.when(i == 0)(ring_and_partner)
         staged(i, -2, gather_stage, 1)
         staged(i, -4, send_stage, 3)
-
-        @pl.when(i == 1)
-        def _():
-            build_all_mix()
-
+        pl.when(i == 1)(turn_tables)
+        staged(i, 2, weight_stage, 0)
         staged(i, 4, mix_stage, 0)
         staged(i, 5, drain_stage, 0)
         return carry
@@ -489,6 +487,7 @@
             vmem(2, nz, pair, half), vmem(2, nz, pair, half),
             vmem(nz, 2, pair, half),
             vmem(nz, 2 * pair, half),
+            vmem(2, rows, 128, dtype=F32),
             vmem(nz, 2, 2, rows, 2 * pair),
             vmem(rows, quarter, dtype=F32),
             dma((2 + ny,)), *each(2), dma, dma, *each(nz), *each(nz),

time: 163 us -> 170 us (1.043)
  Pallas kernels: 162 us -> 168 us
    pallas_call x1, Pallas kernels: 162 us -> 168 us  [on_device(): pl.pallas_call(functools.partial(moe_kernel, nsec, nz, ny), out_shape=jax...]
where the time goes in v9:
time: 170 us
  Pallas kernels  168 us (99%)
    pallas_call x1, Pallas kernels, on_device(): pl.pallas_call(functools.partial(moe_kernel, nsec, nz, ny), out_shape=jax...  168 us

profile of v9, /device:TPU:1, one launch (start us, length us, event | category | flops | bytes accessed | tf_op | source)
XLA Modules:
  0.0 169.9 jit_solution(17316993025412788936)
XLA Ops:
  0.0 168.2 %shard_map.64 = bf16[128,1024]{1,0:T(8,128)(2,1)} custom-call(bf16[128,1024]{1,0:T(8,128)(2,1)} %bitcast.15, s32[8,128]{1,0:T(8,128)} %bitcast.16, f32[8,128]{1,0:T(8,128)} %bitcast.17, bf16[4096,384]{1,0:T(8,128)(2,1)} %bitcast.12, bf16[4096,384]{1,0:T(8,128)(2,1)} %bitcast.13, bf16[384,4096]{1,0:T(8,128)(2,1)} %bitcast.14), custom_call_target="tpu_custom_call" | custom-call | flops 10871635968 | bytes 9437184 | tf_op jit(solution)/shard_map/pallas_call | solution.py:469
  168.2 1.7 copy.8
